TPU v7x, 32 devices: a whole 2x2x4 slice. The times are simulated.
32 devices in a mesh: groups: 2 (over x), section: 16 (over z, y, core).
Axes of the slice: x: 2, y: 2, z: 4, core: 2. Of those that a mesh axis runs over, the one named last changes fastest.
Arguments:
- tiles: float32 [32, 256, 256], P(('groups', 'section')), parts along dimension 0, may hold values from -6 to 6
- partners: int32 [32, 3], P(('groups', 'section')), parts along dimension 0, may hold values from 0 to 1, as said below
Outputs:
- shifts: float32 [32, 3, 9, 1024], P(('groups', 'section')), parts along dimension 0
There are 2 independent parts, one for each index of `groups`. A program takes and returns all parts, laid end to end along the dimension named above; each array names one. Nothing has to cross between parts.
Inputs may be any that keep to these rules, and one draw needn't show every extreme that they name: `partners`: every section lists at least one partner offset.
All inputs are finite; a program needn't handle non-finite values.
Results may differ from a plain program's by a relative error of at most 0.00007.
Values sent between devices are 32-bit elements; how exact they have to be, the bound alone decides.
A program may use at most 64 MiB of HBM per device.

v0:
```python
import functools
import math

import jax
import jax.numpy as jnp
import ml_dtypes
import numpy as np
from jax import lax
from jax.experimental import pallas as pl
from jax.experimental.pallas import tpu as pltpu
from jax.sharding import PartitionSpec as P

PATCH = 128
REACH = 3
CROP = 32
HALF = PATCH // 2
ROWS = 80
CHUNKS = 2
BF = jnp.bfloat16


def split_table(table):
    high = table.astype(ml_dtypes.bfloat16)
    low = (table - high.astype(np.float64)).astype(ml_dtypes.bfloat16)
    return high, low


def tables():
    x = np.arange(PATCH)
    k = np.arange(ROWS)
    live = (k <= HALF)[:, None]
    turn = 2.0 * math.pi / PATCH
    angle = (k[:, None] * x[None, :] % PATCH) * turn
    column = np.concatenate([np.cos(angle) * live, np.sin(angle) * live], 0)
    high, low = split_table(column)
    first = np.concatenate(
        [np.concatenate([high, high], 1), np.concatenate([low, np.zeros_like(low)], 1)], 0
    )
    angle = (x[:, None] * x[None, :] % PATCH) * turn
    cosine, sine = np.cos(angle), np.sin(angle)
    second = np.stack(split_table(np.block([[cosine, -sine], [-sine, -cosine]])))
    kept = np.arange(CROP) - CROP // 2
    angle = (x[:, None] * np.tile(kept, PATCH // CROP)[None, :] % PATCH) * turn
    cosine, sine = np.cos(angle), np.sin(angle)
    third = np.stack(split_table(np.block([[cosine, sine], [-sine, cosine]])))
    weight = np.where(k == 0, 1.0, np.where(k < HALF, 2.0, np.where(k == HALF, 1.0, 0.0)))
    angle = (kept[:, None] * k[None, :] % PATCH) * turn
    last = np.concatenate([np.cos(angle) * weight, -np.sin(angle) * weight], 1) / float(PATCH**3)
    fourth = np.concatenate(split_table(last), 0)
    return first, second, third, fourth


def split(value):
    high = value.astype(BF)
    return high, (value - high.astype(jnp.float32)).astype(BF)


def dot(a, b):
    return jnp.dot(a, b, preferred_element_type=jnp.float32)


def kernel(total, grid, tile_ref, first, second, third, fourth, out_ref,
           slots, mine, other, seg_h, seg_l, lined, send_sem, recv_sem, forward_sem):
    me = lax.axis_index("section")
    even = lax.rem(me, 2) == 0
    odd = jnp.logical_not(even)
    piece = tile_ref.shape[0] // CHUNKS
    partner = jnp.where(even, me + 1, me - 1)

    barrier = pltpu.get_barrier_semaphore()
    writers = [
        (me + 2 < total, me + 2),
        (even & (me + 1 < total), me + 1),
        (odd & (me + 3 < total), me + 3),
        (odd & (me + 1 < total), me - 1),
    ]
    targets = [
        me >= 2,
        even & (me >= 3),
        odd,
        even & (me + 2 < total),
    ]
    for wanted, device in writers:
        @pl.when(wanted)
        def _():
            pl.semaphore_signal(barrier, inc=1, device_id={"section": device},
                                device_id_type=pl.DeviceIdType.MESH)
    pl.semaphore_wait(barrier, sum(t.astype(jnp.int32) for t in targets))

    def rows(c):
        return pl.ds(c * piece, piece)

    def send(c, slot, device, which):
        return pltpu.make_async_remote_copy(
            src_ref=tile_ref.at[rows(c)], dst_ref=slots.at[slot, rows(c)],
            send_sem=send_sem.at[which, c], recv_sem=recv_sem.at[slot, c],
            device_id={"section": device}, device_id_type=pl.DeviceIdType.MESH)

    def forward_copy(c, slot):
        return pltpu.make_async_remote_copy(
            src_ref=slots.at[1, rows(c)], dst_ref=slots.at[slot, rows(c)],
            send_sem=forward_sem.at[c], recv_sem=recv_sem.at[slot, c],
            device_id={"section": partner}, device_id_type=pl.DeviceIdType.MESH)

    def arrived(c, slot):
        pltpu.make_async_remote_copy(
            src_ref=tile_ref.at[rows(c)], dst_ref=slots.at[slot, rows(c)],
            send_sem=send_sem.at[0, c], recv_sem=recv_sem.at[slot, c],
            device_id={"section": partner}, device_id_type=pl.DeviceIdType.MESH).wait_recv()

    sends = [(me >= 2, 1, me - 2, 0), (even & (me >= 3), 2, me - 3, 1), (odd, 0, me - 1, 1)]
    for c in range(CHUNKS):
        for wanted, slot, device, which in sends:
            @pl.when(wanted)
            def _():
                send(c, slot, device, which).start()

    def transform(read, into):
        for i in range(grid):
            highs, lows = [], []
            for j in range(grid):
                block = read(pl.ds(i * HALF, PATCH), pl.ds(j * HALF, PATCH))
                middle = jnp.sum(jnp.sum(block, 0, keepdims=True), 1, keepdims=True) * (1.0 / PATCH**2)
                centred = block - middle
                spread = jnp.sum(jnp.sum(centred * centred, 0, keepdims=True), 1, keepdims=True)
                scale = 1.0 / jnp.sqrt(spread * (1.0 / PATCH**2) + 1e-06)
                high, low = split(centred * scale)
                highs.append(high)
                lows.append(low)
            stacked = jnp.concatenate(
                [jnp.concatenate(highs, 1), jnp.concatenate(lows, 1)], 0)
            seg = dot(first[...], stacked)
            seg = seg[:2 * ROWS] + seg[2 * ROWS:]
            for j in range(grid):
                at = pl.ds((i * grid + j) * ROWS, ROWS)
                part = seg[:, j * PATCH:(j + 1) * PATCH]
                high, low = split(jnp.concatenate([part[:ROWS], part[ROWS:]], 1))
                seg_h[at] = high
                seg_l[at] = low
        high = seg_h[...]
        into[...] = dot(high, second[0]) + dot(seg_l[...], second[0]) + dot(high, second[1])

    def correlate(slot):
        a_r, a_i = mine[:, :PATCH], mine[:, PATCH:]
        b_r, b_i = other[:, :PATCH], other[:, PATCH:]
        high, low = split(jnp.concatenate([a_r * b_r + a_i * b_i, a_r * b_i - a_i * b_r], 1))
        half = dot(high, third[0]) + dot(low, third[0]) + dot(high, third[1])
        highs, lows = [], []
        for p in range(grid * grid):
            part = half[p * ROWS:(p + 1) * ROWS]
            high, low = split(jnp.concatenate([part[:, :PATCH], part[:, PATCH:]], 0))
            highs.append(high)
            lows.append(low)
        table = fourth[...]
        done = dot(table, jnp.concatenate(highs, 1))
        done = done[:CROP] + done[CROP:] + dot(table[:CROP], jnp.concatenate(lows, 1))
        for p in range(grid * grid):
            lined[pl.ds(p * CROP, CROP)] = done[:, p * PATCH:(p + 1) * PATCH]
        lane = lax.broadcasted_iota(jnp.int32, (grid * grid, PATCH), 1) // CROP
        per = PATCH // CROP
        for g in range(CROP // per):
            line = lined[pl.ds(g * per, grid * grid, stride=CROP)]
            for q in range(1, per):
                line = jnp.where(lane == q, lined[pl.ds(g * per + q, grid * grid, stride=CROP)], line)
            out_ref[slot, :, g * PATCH:(g + 1) * PATCH] = line

    transform(lambda r, c: tile_ref[r, c], mine)

    def receive(slot):
        for c in range(CHUNKS):
            arrived(c, slot)

    def work(slot):
        transform(lambda r, c: slots[slot, r, c], other)
        correlate(slot)

    @pl.when(even & (me + 1 < total))
    def _():
        receive(0)

    @pl.when(even & (me + 2 < total))
    def _():
        for c in range(CHUNKS):
            arrived(c, 1)
            forward_copy(c, 0).start()

    @pl.when(odd & (me + 2 < total))
    def _():
        for c in range(CHUNKS):
            arrived(c, 1)
            forward_copy(c, 2).start()

    @pl.when(odd & (me + 1 < total))
    def _():
        receive(0)

    for slot in range(REACH):
        @pl.when(me + slot + 1 < total)
        def _():
            if slot == 2:
                receive(2)
            work(slot)

        @pl.when(me + slot + 1 >= total)
        def _():
            out_ref[slot] = jnp.zeros(out_ref.shape[1:], jnp.float32)

    for c in range(CHUNKS):
        for wanted, slot, device, which in sends:
            @pl.when(wanted)
            def _():
                send(c, slot, device, which).wait_send()

        @pl.when(me + 2 < total)
        def _():
            forward_copy(c, 0).wait_send()


def body(tiles, partners):
    side = tiles.shape[-1]
    grid = side // HALF - 1
    total = lax.axis_size("section")
    count = grid * grid
    vmem = pl.BlockSpec(memory_space=pltpu.VMEM)
    result = pl.pallas_call(
        functools.partial(kernel, total, grid),
        out_shape=jax.ShapeDtypeStruct((REACH, count, CROP * CROP), jnp.float32),
        in_specs=[vmem] * 5,
        out_specs=vmem,
        scratch_shapes=[
            pltpu.VMEM((REACH, side, side), jnp.float32),
            pltpu.VMEM((count * ROWS, 2 * PATCH), jnp.float32),
            pltpu.VMEM((count * ROWS, 2 * PATCH), jnp.float32),
            pltpu.VMEM((count * ROWS, 2 * PATCH), BF),
            pltpu.VMEM((count * ROWS, 2 * PATCH), BF),
            pltpu.VMEM((count * CROP, PATCH), jnp.float32),
            pltpu.SemaphoreType.DMA((2, CHUNKS)),
            pltpu.SemaphoreType.DMA((REACH, CHUNKS)),
            pltpu.SemaphoreType.DMA((CHUNKS,)),
        ],
        compiler_params=pltpu.CompilerParams(
            collective_id=0, has_side_effects=True, vmem_limit_bytes=48 * 1024 * 1024
        ),
    )(tiles[0], *[jnp.asarray(t) for t in tables()])
    position = lax.axis_index("section")
    offsets = jnp.arange(REACH, dtype=jnp.int32) + 1
    listed = (partners[0] == 1) & (position + offsets < total)
    return jnp.where(listed[:, None, None], result, 0.0)[None]


def solution(mesh):
    in_specs = (P(("groups", "section"), None, None), P(("groups", "section"), None))
    out_specs = P(("groups", "section"), None, None, None)
    return jax.shard_map(body, mesh=mesh, in_specs=in_specs, out_specs=out_specs, check_vma=False)
```

profile of v0, /device:TPU:7, one launch (start us, length us, event | category | flops | bytes accessed | tf_op | source)
XLA Modules:
  0.0 25.1 jit_solution(10384060109420599067)
XLA Ops:
  0.0 0.0 copy-start.5
  0.0 0.7 %copy-done.5 = s32[1,3]{1,0:T(1,128)S(1)} copy-done((s32[1,3]{1,0:T(1,128)S(1)}, s32[1,3]{1,0:T(1,128)}, u32[]{:S(2)}) %copy-start.5) | copy-done | bytes 36
  0.7 0.0 copy-start
  0.7 0.9 %copy-done = f32[1,256,256]{2,1,0:T(8,128)S(1)} copy-done((f32[1,256,256]{2,1,0:T(8,128)S(1)}, f32[1,256,256]{2,1,0:T(8,128)}, u32[]{:S(2)}) %copy-start) | copy-done | bytes 262168
  1.6 0.0 copy-start.1
  1.6 0.9 %copy-done.1 = bf16[2,256,256]{2,1,0:T(8,128)(2,1)S(1)} copy-done((bf16[2,256,256]{2,1,0:T(8,128)(2,1)S(1)}, bf16[2,256,256]{2,1,0:T(8,128)(2,1)}, u32[]{:S(2)}) %copy-start.1) | copy-done | bytes 262168
  2.6 0.0 copy-start.2
  2.6 0.9 %copy-done.2 = bf16[2,256,256]{2,1,0:T(8,128)(2,1)S(1)} copy-done((bf16[2,256,256]{2,1,0:T(8,128)(2,1)S(1)}, bf16[2,256,256]{2,1,0:T(8,128)(2,1)}, u32[]{:S(2)}) %copy-start.2) | copy-done | bytes 262168
  3.5 0.0 copy-start.3
  3.5 0.9 %copy-done.3 = bf16[320,256]{1,0:T(8,128)(2,1)S(1)} copy-done((bf16[320,256]{1,0:T(8,128)(2,1)S(1)}, bf16[320,256]{1,0:T(8,128)(2,1)}, u32[]{:S(2)}) %copy-start.3) | copy-done | bytes 163864
  4.4 0.0 copy-start.4
  4.4 0.8 %copy-done.4 = bf16[64,160]{1,0:T(8,128)(2,1)S(1)} copy-done((bf16[64,160]{1,0:T(8,128)(2,1)S(1)}, bf16[64,160]{1,0:T(8,128)(2,1)}, u32[]{:S(2)}) %copy-start.4) | copy-done | bytes 20504
  5.2 19.1 %shard_map.64 = f32[3,9,1024]{2,1,0:T(8,128)S(1)} custom-call(f32[256,256]{1,0:T(8,128)S(1)} %bitcast.5, bf16[320,256]{1,0:T(8,128)(2,1)S(1)} %copy-done.3, bf16[2,256,256]{2,1,0:T(8,128)(2,1)S(1)} %copy-done.2, bf16[2,256,256]{2,1,0:T(8,128)(2,1)S(1)} %copy-done.1, bf16[64,160]{1,0:T(8,128)(2,1)S(1)} %copy-done.4), custom_call_target="tpu_custom_call" | custom-call | tf_op jit(solution)/shard_map/pallas_call | solution.py:225
  24.3 0.1 select_bitcast_fusion
  24.3 0.8 %copy.7 = f32[1,3,9,1024]{3,0,2,1:T(1,128)} copy(f32[1,3,9,1024]{3,2,1,0:T(8,128)S(1)} %select_bitcast_fusion) | data formatting | bytes 221184 | tf_op jit(solution)/shard_map/broadcast_in_dim | solution.py:248
  (1 shorter events, 0.0 us)
Async XLA Ops:
  0.0 0.7 %copy-start.5 = (s32[1,3]{1,0:T(1,128)S(1)}, s32[1,3]{1,0:T(1,128)}, u32[]{:S(2)}) copy-start(s32[1,3]{1,0:T(1,128)} %param.7) | copy-start | bytes 40
  0.7 0.9 %copy-start = (f32[1,256,256]{2,1,0:T(8,128)S(1)}, f32[1,256,256]{2,1,0:T(8,128)}, u32[]{:S(2)}) copy-start(f32[1,256,256]{2,1,0:T(8,128)} %param.6) | copy-start | bytes 786436
  1.6 0.9 %copy-start.1 = (bf16[2,256,256]{2,1,0:T(8,128)(2,1)S(1)}, bf16[2,256,256]{2,1,0:T(8,128)(2,1)}, u32[]{:S(2)}) copy-start(bf16[2,256,256]{2,1,0:T(8,128)(2,1)} %constant.20.clone.third) | copy-start | bytes 786436
  2.6 0.9 %copy-start.2 = (bf16[2,256,256]{2,1,0:T(8,128)(2,1)S(1)}, bf16[2,256,256]{2,1,0:T(8,128)(2,1)}, u32[]{:S(2)}) copy-start(bf16[2,256,256]{2,1,0:T(8,128)(2,1)} %constant.19.clone.second) | copy-start | bytes 786436
  3.5 0.9 %copy-start.3 = (bf16[320,256]{1,0:T(8,128)(2,1)S(1)}, bf16[320,256]{1,0:T(8,128)(2,1)}, u32[]{:S(2)}) copy-start(bf16[320,256]{1,0:T(8,128)(2,1)} %constant.18.clone.first) | copy-start | bytes 491524
  4.4 0.8 %copy-start.4 = (bf16[64,160]{1,0:T(8,128)(2,1)S(1)}, bf16[64,160]{1,0:T(8,128)(2,1)}, u32[]{:S(2)}) copy-start(bf16[64,160]{1,0:T(8,128)(2,1)} %constant.21.clone.fourth) | copy-start | bytes 61444
where the time goes:
time: 25.4 us; the launch traced here: 25.1 us
  Pallas kernels  19.1 us (75%)
  local copies, waits for them, and re-layouts  5.93 us (23%)
    pallas_call x1, Pallas kernels, body(): pl.pallas_call(functools.partial(kernel, total, grid), out_shape=jax.Shap...  19.1 us
    unnamed x12, local copies, waits for them, and re-layouts  5.18 us
    broadcast_in_dim x1, local copies, waits for them, and re-layouts, body(): return jnp.where(listed[:, None, None], result, 0.0)[None]  0.76 us

commit v1 on v0

--- a/solution.py
+++ b/solution.py
@@ -23,6 +23,11 @@
     high = table.astype(ml_dtypes.bfloat16)
     low = (table - high.astype(np.float64)).astype(ml_dtypes.bfloat16)
     return high, low
+
+
+def thrice(table):
+    high, low = split_table(table)
+    return np.concatenate([high, high, low], 0)
 
 
 def tables():
@@ -38,11 +43,11 @@
     )
     angle = (x[:, None] * x[None, :] % PATCH) * turn
     cosine, sine = np.cos(angle), np.sin(angle)
-    second = np.stack(split_table(np.block([[cosine, -sine], [-sine, -cosine]])))
+    second = thrice(np.block([[cosine, -sine], [-sine, -cosine]]))
     kept = np.arange(CROP) - CROP // 2
     angle = (x[:, None] * np.tile(kept, PATCH // CROP)[None, :] % PATCH) * turn
     cosine, sine = np.cos(angle), np.sin(angle)
-    third = np.stack(split_table(np.block([[cosine, sine], [-sine, cosine]])))
+    third = thrice(np.block([[cosine, sine], [-sine, cosine]]))
     weight = np.where(k == 0, 1.0, np.where(k < HALF, 2.0, np.where(k == HALF, 1.0, 0.0)))
     angle = (kept[:, None] * k[None, :] % PATCH) * turn
     last = np.concatenate([np.cos(angle) * weight, -np.sin(angle) * weight], 1) / float(PATCH**3)
@@ -59,13 +64,23 @@
     return jnp.dot(a, b, preferred_element_type=jnp.float32)
 
 
-def kernel(total, grid, tile_ref, first, second, third, fourth, out_ref,
-           slots, mine, other, seg_h, seg_l, lined, send_sem, recv_sem, forward_sem):
+def kernel(total, grid, tile_ref, partners_ref, first_ref, second_ref, third_ref, fourth_ref, out_ref,
+           own, partners, first, second, third, fourth, load_sem, slots, mine, other, seg_h, seg_l, lined, send_sem, recv_sem, forward_sem):
     me = lax.axis_index("section")
     even = lax.rem(me, 2) == 0
     odd = jnp.logical_not(even)
     piece = tile_ref.shape[0] // CHUNKS
     partner = jnp.where(even, me + 1, me - 1)
+    lines = out_ref.shape[0] // REACH
+
+    loads = [
+        pltpu.make_async_copy(source, into, load_sem.at[n])
+        for n, (source, into) in enumerate([
+            (tile_ref, own), (first_ref, first), (second_ref, second),
+            (third_ref, third), (fourth_ref, fourth), (partners_ref, partners)])
+    ]
+    for load in loads:
+        load.start()
 
     barrier = pltpu.get_barrier_semaphore()
     writers = [
@@ -138,13 +153,13 @@
                 seg_h[at] = high
                 seg_l[at] = low
         high = seg_h[...]
-        into[...] = dot(high, second[0]) + dot(seg_l[...], second[0]) + dot(high, second[1])
+        into[...] = dot(jnp.concatenate([high, seg_l[...], high], 1), second[...])
 
     def correlate(slot):
         a_r, a_i = mine[:, :PATCH], mine[:, PATCH:]
         b_r, b_i = other[:, :PATCH], other[:, PATCH:]
         high, low = split(jnp.concatenate([a_r * b_r + a_i * b_i, a_r * b_i - a_i * b_r], 1))
-        half = dot(high, third[0]) + dot(low, third[0]) + dot(high, third[1])
+        half = dot(jnp.concatenate([high, low, high], 1), third[...])
         highs, lows = [], []
         for p in range(grid * grid):
             part = half[p * ROWS:(p + 1) * ROWS]
@@ -158,52 +173,37 @@
             lined[pl.ds(p * CROP, CROP)] = done[:, p * PATCH:(p + 1) * PATCH]
         lane = lax.broadcasted_iota(jnp.int32, (grid * grid, PATCH), 1) // CROP
         per = PATCH // CROP
+        listed = partners[0, slot] == 1
         for g in range(CROP // per):
             line = lined[pl.ds(g * per, grid * grid, stride=CROP)]
             for q in range(1, per):
                 line = jnp.where(lane == q, lined[pl.ds(g * per + q, grid * grid, stride=CROP)], line)
-            out_ref[slot, :, g * PATCH:(g + 1) * PATCH] = line
-
-    transform(lambda r, c: tile_ref[r, c], mine)
-
-    def receive(slot):
-        for c in range(CHUNKS):
-            arrived(c, slot)
-
-    def work(slot):
-        transform(lambda r, c: slots[slot, r, c], other)
-        correlate(slot)
-
-    @pl.when(even & (me + 1 < total))
-    def _():
-        receive(0)
-
-    @pl.when(even & (me + 2 < total))
-    def _():
-        for c in range(CHUNKS):
-            arrived(c, 1)
-            forward_copy(c, 0).start()
-
-    @pl.when(odd & (me + 2 < total))
-    def _():
-        for c in range(CHUNKS):
-            arrived(c, 1)
-            forward_copy(c, 2).start()
-
-    @pl.when(odd & (me + 1 < total))
-    def _():
-        receive(0)
-
-    for slot in range(REACH):
-        @pl.when(me + slot + 1 < total)
-        def _():
-            if slot == 2:
-                receive(2)
-            work(slot)
-
-        @pl.when(me + slot + 1 >= total)
-        def _():
-            out_ref[slot] = jnp.zeros(out_ref.shape[1:], jnp.float32)
+            out_ref[pl.ds(slot * lines + g, grid * grid, stride=CROP // per)] = jnp.where(listed, line, 0.0)
+
+    loads[0].wait()
+    loads[1].wait()
+    loads[2].wait()
+    transform(lambda r, c: own[r, c], mine)
+    loads[3].wait()
+    loads[4].wait()
+    loads[5].wait()
+
+    for step in range(REACH):
+        slot = jnp.where(even, step, REACH - 1 - step)
+        here = me + slot + 1 < total
+
+        @pl.when(here)
+        def _():
+            for c in range(CHUNKS):
+                arrived(c, slot)
+                if step == 1:
+                    forward_copy(c, jnp.where(even, 0, 2)).start()
+            transform(lambda r, c: slots[slot, r, c], other)
+            correlate(slot)
+
+        @pl.when(jnp.logical_not(here))
+        def _():
+            out_ref[pl.ds(slot * lines, lines)] = jnp.zeros((lines, PATCH), jnp.float32)
 
     for c in range(CHUNKS):
         for wanted, slot, device, which in sends:
@@ -221,13 +221,19 @@
     grid = side // HALF - 1
     total = lax.axis_size("section")
     count = grid * grid
+    lines = count * CROP * CROP // PATCH
+    constants = tables()
     vmem = pl.BlockSpec(memory_space=pltpu.VMEM)
     result = pl.pallas_call(
         functools.partial(kernel, total, grid),
-        out_shape=jax.ShapeDtypeStruct((REACH, count, CROP * CROP), jnp.float32),
-        in_specs=[vmem] * 5,
+        out_shape=jax.ShapeDtypeStruct((REACH * lines, PATCH), jnp.float32),
+        in_specs=[pl.BlockSpec(memory_space=pltpu.HBM)] * 6,
         out_specs=vmem,
         scratch_shapes=[
+            pltpu.VMEM((side, side), jnp.float32),
+            pltpu.SMEM((1, REACH), jnp.int32),
+            *[pltpu.VMEM(t.shape, BF) for t in constants],
+            pltpu.SemaphoreType.DMA((6,)),
             pltpu.VMEM((REACH, side, side), jnp.float32),
             pltpu.VMEM((count * ROWS, 2 * PATCH), jnp.float32),
             pltpu.VMEM((count * ROWS, 2 * PATCH), jnp.float32),
@@ -239,13 +245,10 @@
             pltpu.SemaphoreType.DMA((CHUNKS,)),
         ],
         compiler_params=pltpu.CompilerParams(
-            collective_id=0, has_side_effects=True, vmem_limit_bytes=48 * 1024 * 1024
+            collective_id=0, has_side_effects=True, vmem_limit_bytes=63_000_000
         ),
-    )(tiles[0], *[jnp.asarray(t) for t in tables()])
-    position = lax.axis_index("section")
-    offsets = jnp.arange(REACH, dtype=jnp.int32) + 1
-    listed = (partners[0] == 1) & (position + offsets < total)
-    return jnp.where(listed[:, None, None], result, 0.0)[None]
+    )(tiles[0], partners, *[jnp.asarray(t) for t in constants])
+    return result.reshape(1, REACH, count, CROP * CROP)
 
 
 def solution(mesh):

time: 25.4 us -> 22.4 us (0.88)
  the two profiles are of different devices: /device:TPU:7 before, /device:TPU:1 now
where the time goes in v1:
time: 22.4 us; the launch traced here: 22.3 us
  Pallas kernels  20.7 us (92%)
  local copies, waits for them, and re-layouts  1.55 us (7%)
    pallas_call x1, Pallas kernels, body(): pl.pallas_call(functools.partial(kernel, total, grid), out_shape=jax.Shap...  20.7 us
    unnamed x1, local copies, waits for them, and re-layouts  1.55 us

profile of v1, /device:TPU:1, one launch (start us, length us, event | category | flops | bytes accessed | tf_op | source)
XLA Modules:
  0.0 22.3 jit_solution(1166886399585283700)
XLA Ops:
  0.0 20.7 %shard_map.64 = f32[216,128]{1,0:T(8,128)} custom-call(f32[256,256]{1,0:T(8,128)} %bitcast.3, s32[1,3]{1,0:T(1,128)} %partners_ref.1, bf16[320,256]{1,0:T(8,128)(2,1)} %constant.8.clone.first_ref, bf16[768,256]{1,0:T(8,128)(2,1)} %constant.9.clone.second_ref, bf16[768,256]{1,0:T(8,128)(2,1)} %constant.10.clone.third_ref, ...), custom_call_target="tpu_custom_call" | custom-call | tf_op jit(solution)/shard_map/pallas_call | solution.py:227
  20.7 1.5 %copy.10 = f32[1,3,9,1024]{3,0,2,1:T(1,128)} copy(f32[1,3,9,1024]{3,0,2,1:T(1,128)} %bitcast.2) | data formatting | bytes 221184

commit v2 on v1

--- a/solution.py
+++ b/solution.py
@@ -50,7 +50,7 @@
     third = thrice(np.block([[cosine, sine], [-sine, cosine]]))
     weight = np.where(k == 0, 1.0, np.where(k < HALF, 2.0, np.where(k == HALF, 1.0, 0.0)))
     angle = (kept[:, None] * k[None, :] % PATCH) * turn
-    last = np.concatenate([np.cos(angle) * weight, -np.sin(angle) * weight], 1) / float(PATCH**3)
+    last = np.concatenate([np.cos(angle) * weight, -np.sin(angle) * weight], 1) / float(PATCH**2)
     fourth = np.concatenate(split_table(last), 0)
     return first, second, third, fourth
 
@@ -65,7 +65,7 @@
 
 
 def kernel(total, grid, tile_ref, partners_ref, first_ref, second_ref, third_ref, fourth_ref, out_ref,
-           own, partners, first, second, third, fourth, load_sem, slots, mine, other, seg_h, seg_l, lined, send_sem, recv_sem, forward_sem):
+           partners, first, second, third, fourth, load_sem, slots, spectra, seg_h, seg_l, lined, send_sem, recv_sem, forward_sem):
     me = lax.axis_index("section")
     even = lax.rem(me, 2) == 0
     odd = jnp.logical_not(even)
@@ -76,7 +76,7 @@
     loads = [
         pltpu.make_async_copy(source, into, load_sem.at[n])
         for n, (source, into) in enumerate([
-            (tile_ref, own), (first_ref, first), (second_ref, second),
+            (tile_ref, slots.at[REACH]), (first_ref, first), (second_ref, second),
             (third_ref, third), (fourth_ref, fourth), (partners_ref, partners)])
     ]
     for load in loads:
@@ -156,8 +156,8 @@
         into[...] = dot(jnp.concatenate([high, seg_l[...], high], 1), second[...])
 
     def correlate(slot):
-        a_r, a_i = mine[:, :PATCH], mine[:, PATCH:]
-        b_r, b_i = other[:, :PATCH], other[:, PATCH:]
+        a_r, a_i = spectra[0, :, :PATCH], spectra[0, :, PATCH:]
+        b_r, b_i = spectra[1, :, :PATCH], spectra[1, :, PATCH:]
         high, low = split(jnp.concatenate([a_r * b_r + a_i * b_i, a_r * b_i - a_i * b_r], 1))
         half = dot(jnp.concatenate([high, low, high], 1), third[...])
         highs, lows = [], []
@@ -180,30 +180,36 @@
                 line = jnp.where(lane == q, lined[pl.ds(g * per + q, grid * grid, stride=CROP)], line)
             out_ref[pl.ds(slot * lines + g, grid * grid, stride=CROP // per)] = jnp.where(listed, line, 0.0)
 
-    loads[0].wait()
-    loads[1].wait()
-    loads[2].wait()
-    transform(lambda r, c: own[r, c], mine)
-    loads[3].wait()
-    loads[4].wait()
-    loads[5].wait()
-
-    for step in range(REACH):
-        slot = jnp.where(even, step, REACH - 1 - step)
-        here = me + slot + 1 < total
-
-        @pl.when(here)
+    for load in loads:
+        load.wait()
+
+    def turn(step, carry):
+        slot = jnp.where(step == 0, REACH, jnp.where(even, step - 1, REACH - step))
+        here = (step == 0) | (me + slot + 1 < total)
+
+        @pl.when(here & (step > 0))
         def _():
             for c in range(CHUNKS):
                 arrived(c, slot)
-                if step == 1:
+
+                @pl.when(step == 2)
+                def _():
                     forward_copy(c, jnp.where(even, 0, 2)).start()
-            transform(lambda r, c: slots[slot, r, c], other)
+
+        @pl.when(here)
+        def _():
+            transform(lambda r, c: slots[slot, r, c], spectra.at[jnp.minimum(step, 1)])
+
+        @pl.when(here & (step > 0))
+        def _():
             correlate(slot)
 
         @pl.when(jnp.logical_not(here))
         def _():
-            out_ref[pl.ds(slot * lines, lines)] = jnp.zeros((lines, PATCH), jnp.float32)
+            out_ref[pl.ds(pl.multiple_of(slot * lines, 8), lines)] = jnp.zeros((lines, PATCH), jnp.float32)
+        return carry
+
+    lax.fori_loop(0, REACH + 1, turn, 0)
 
     for c in range(CHUNKS):
         for wanted, slot, device, which in sends:
@@ -230,13 +236,11 @@
         in_specs=[pl.BlockSpec(memory_space=pltpu.HBM)] * 6,
         out_specs=vmem,
         scratch_shapes=[
-            pltpu.VMEM((side, side), jnp.float32),
             pltpu.SMEM((1, REACH), jnp.int32),
             *[pltpu.VMEM(t.shape, BF) for t in constants],
             pltpu.SemaphoreType.DMA((6,)),
-            pltpu.VMEM((REACH, side, side), jnp.float32),
-            pltpu.VMEM((count * ROWS, 2 * PATCH), jnp.float32),
-            pltpu.VMEM((count * ROWS, 2 * PATCH), jnp.float32),
+            pltpu.VMEM((REACH + 1, side, side), jnp.float32),
+            pltpu.VMEM((2, count * ROWS, 2 * PATCH), jnp.float32),
             pltpu.VMEM((count * ROWS, 2 * PATCH), BF),
             pltpu.VMEM((count * ROWS, 2 * PATCH), BF),
             pltpu.VMEM((count * CROP, PATCH), jnp.float32),
@@ -248,6 +252,7 @@
             collective_id=0, has_side_effects=True, vmem_limit_bytes=63_000_000
         ),
     )(tiles[0], partners, *[jnp.asarray(t) for t in constants])
+    result = lax.optimization_barrier(result * (1.0 / PATCH))
     return result.reshape(1, REACH, count, CROP * CROP)
 
 

time: 22.4 us -> 22 us (0.982)
  other arithmetic: 0 us -> 1.55 us
  local copies, waits for them, and re-layouts: 1.55 us -> 0 us
  Pallas kernels: 20.7 us -> 20.3 us
    mul x0 -> x1, other arithmetic: none -> 1.55 us  [body(): result = lax.optimization_barrier(result * (1.0 / PATCH))]
    unnamed x1 -> x0, local copies, waits for them, and re-layouts: 1.55 us -> none
    pallas_call x1, Pallas kernels: 20.7 us -> 20.3 us  [body(): pl.pallas_call(functools.partial(kernel, total, grid), out_shape=jax.Shap...]
where the time goes in v2:
time: 22 us; the launch traced here: 21.8 us
  Pallas kernels  20.3 us (92%)
  other arithmetic  1.55 us (7%)
    pallas_call x1, Pallas kernels, body(): pl.pallas_call(functools.partial(kernel, total, grid), out_shape=jax.Shap...  20.3 us
    mul x1, other arithmetic, body(): result = lax.optimization_barrier(result * (1.0 / PATCH))  1.55 us

profile of v2, /device:TPU:1, one launch (start us, length us, event | category | flops | bytes accessed | tf_op | source)
XLA Modules:
  0.0 21.8 jit_solution(14925937938525148903)
XLA Ops:
  0.0 20.3 %shard_map.64 = f32[216,128]{1,0:T(8,128)} custom-call(f32[256,256]{1,0:T(8,128)} %bitcast.2, s32[1,3]{1,0:T(1,128)} %partners_ref.1, bf16[320,256]{1,0:T(8,128)(2,1)} %constant.10.clone.first_ref, bf16[768,256]{1,0:T(8,128)(2,1)} %constant.11.clone.second_ref, bf16[768,256]{1,0:T(8,128)(2,1)} %constant.12.clone.third_ref, ...), custom_call_target="tpu_custom_call" | custom-call | tf_op jit(solution)/shard_map/pallas_call | solution.py:233
  20.3 1.6 %broadcast_multiply_fusion = f32[216,128]{1,0:T(8,128)} fusion(f32[216,128]{1,0:T(8,128)} %shard_map.64), kind=kLoop, calls=%fused_computation | loop fusion | flops 27648 | bytes 221184 | tf_op jit(solution)/shard_map/mul | solution.py:255

commit v3 on v2

--- a/solution.py
+++ b/solution.py
@@ -52,7 +52,8 @@
     angle = (kept[:, None] * k[None, :] % PATCH) * turn
     last = np.concatenate([np.cos(angle) * weight, -np.sin(angle) * weight], 1) / float(PATCH**2)
     fourth = np.concatenate(split_table(last), 0)
-    return first, second, third, fourth
+    fourth = np.pad(fourth, ((0, 0), (0, first.shape[1] - fourth.shape[1])))
+    return np.concatenate([first, fourth], 0), second, third
 
 
 def split(value):
@@ -64,8 +65,8 @@
     return jnp.dot(a, b, preferred_element_type=jnp.float32)
 
 
-def kernel(total, grid, tile_ref, partners_ref, first_ref, second_ref, third_ref, fourth_ref, out_ref,
-           partners, first, second, third, fourth, load_sem, slots, spectra, seg_h, seg_l, lined, send_sem, recv_sem, forward_sem):
+def kernel(total, grid, tile_ref, partners_ref, first_ref, second_ref, third_ref, out_ref,
+           partners, first, second, third, load_sem, slots, spectra, seg_h, seg_l, lined, send_sem, recv_sem, forward_sem):
     me = lax.axis_index("section")
     even = lax.rem(me, 2) == 0
     odd = jnp.logical_not(even)
@@ -77,7 +78,7 @@
         pltpu.make_async_copy(source, into, load_sem.at[n])
         for n, (source, into) in enumerate([
             (tile_ref, slots.at[REACH]), (first_ref, first), (second_ref, second),
-            (third_ref, third), (fourth_ref, fourth), (partners_ref, partners)])
+            (third_ref, third), (partners_ref, partners)])
     ]
     for load in loads:
         load.start()
@@ -124,27 +125,38 @@
             device_id={"section": partner}, device_id_type=pl.DeviceIdType.MESH).wait_recv()
 
     sends = [(me >= 2, 1, me - 2, 0), (even & (me >= 3), 2, me - 3, 1), (odd, 0, me - 1, 1)]
-    for c in range(CHUNKS):
-        for wanted, slot, device, which in sends:
-            @pl.when(wanted)
-            def _():
-                send(c, slot, device, which).start()
+    quick = lax.rem(me // 2, 2) == 1
+
+    def start(which_sends):
+        for c in range(CHUNKS):
+            for wanted, slot, device, which in which_sends:
+                @pl.when(wanted)
+                def _():
+                    send(c, slot, device, which).start()
+
+    start([sends[0], sends[2], (quick & sends[1][0],) + sends[1][1:]])
 
     def transform(read, into):
+        def block(i, j):
+            return read(pl.ds(i * HALF, PATCH), pl.ds(j * HALF, PATCH))
+
+        def mean(value):
+            return jnp.sum(jnp.sum(value, 0, keepdims=True), 1, keepdims=True) * (1.0 / PATCH**2)
+
+        places = [(i, j) for i in range(grid) for j in range(grid)]
+        middles = [mean(block(i, j)) for i, j in places]
+        spreads = [mean((block(i, j) - m) ** 2) for (i, j), m in zip(places, middles)]
+        scales = [1.0 / jnp.sqrt(v + 1e-06) for v in spreads]
         for i in range(grid):
             highs, lows = [], []
             for j in range(grid):
-                block = read(pl.ds(i * HALF, PATCH), pl.ds(j * HALF, PATCH))
-                middle = jnp.sum(jnp.sum(block, 0, keepdims=True), 1, keepdims=True) * (1.0 / PATCH**2)
-                centred = block - middle
-                spread = jnp.sum(jnp.sum(centred * centred, 0, keepdims=True), 1, keepdims=True)
-                scale = 1.0 / jnp.sqrt(spread * (1.0 / PATCH**2) + 1e-06)
-                high, low = split(centred * scale)
+                at = i * grid + j
+                high, low = split((block(i, j) - middles[at]) * scales[at])
                 highs.append(high)
                 lows.append(low)
             stacked = jnp.concatenate(
                 [jnp.concatenate(highs, 1), jnp.concatenate(lows, 1)], 0)
-            seg = dot(first[...], stacked)
+            seg = dot(first[:4 * ROWS], stacked)
             seg = seg[:2 * ROWS] + seg[2 * ROWS:]
             for j in range(grid):
                 at = pl.ds((i * grid + j) * ROWS, ROWS)
@@ -166,7 +178,7 @@
             high, low = split(jnp.concatenate([part[:, :PATCH], part[:, PATCH:]], 0))
             highs.append(high)
             lows.append(low)
-        table = fourth[...]
+        table = first[4 * ROWS:, :2 * ROWS]
         done = dot(table, jnp.concatenate(highs, 1))
         done = done[:CROP] + done[CROP:] + dot(table[:CROP], jnp.concatenate(lows, 1))
         for p in range(grid * grid):
@@ -184,15 +196,20 @@
         load.wait()
 
     def turn(step, carry):
-        slot = jnp.where(step == 0, REACH, jnp.where(even, step - 1, REACH - step))
+        odd_slot = jnp.where(step == REACH, 0, jnp.where(quick, REACH - step, step))
+        slot = jnp.where(step == 0, REACH, jnp.where(even, step - 1, odd_slot))
         here = (step == 0) | (me + slot + 1 < total)
+
+        @pl.when(step == 2)
+        def _():
+            start([(jnp.logical_not(quick) & sends[1][0],) + sends[1][1:]])
 
         @pl.when(here & (step > 0))
         def _():
             for c in range(CHUNKS):
                 arrived(c, slot)
 
-                @pl.when(step == 2)
+                @pl.when(slot == 1)
                 def _():
                     forward_copy(c, jnp.where(even, 0, 2)).start()
 
@@ -233,12 +250,12 @@
     result = pl.pallas_call(
         functools.partial(kernel, total, grid),
         out_shape=jax.ShapeDtypeStruct((REACH * lines, PATCH), jnp.float32),
-        in_specs=[pl.BlockSpec(memory_space=pltpu.HBM)] * 6,
+        in_specs=[pl.BlockSpec(memory_space=pltpu.HBM)] * 5,
         out_specs=vmem,
         scratch_shapes=[
             pltpu.SMEM((1, REACH), jnp.int32),
             *[pltpu.VMEM(t.shape, BF) for t in constants],
-            pltpu.SemaphoreType.DMA((6,)),
+            pltpu.SemaphoreType.DMA((5,)),
             pltpu.VMEM((REACH + 1, side, side), jnp.float32),
             pltpu.VMEM((2, count * ROWS, 2 * PATCH), jnp.float32),
             pltpu.VMEM((count * ROWS, 2 * PATCH), BF),

time: 22 us -> 19.8 us (0.900)
  Pallas kernels: 20.3 us -> 18.1 us
    pallas_call x1, Pallas kernels: 20.3 us -> 18.1 us  [body(): pl.pallas_call(functools.partial(kernel, total, grid), out_shape=jax.Shap...]
where the time goes in v3:
time: 19.8 us; the launch traced here: 19.6 us
  Pallas kernels  18.1 us (91%)
  other arithmetic  1.55 us (8%)
    pallas_call x1, Pallas kernels, body(): pl.pallas_call(functools.partial(kernel, total, grid), out_shape=jax.Shap...  18.1 us
    mul x1, other arithmetic, body(): result = lax.optimization_barrier(result * (1.0 / PATCH))  1.55 us

profile of v3, /device:TPU:1, one launch (start us, length us, event | category | flops | bytes accessed | tf_op | source)
XLA Modules:
  0.0 19.6 jit_solution(17290253236937277159)
XLA Ops:
  0.0 18.1 %shard_map.55 = f32[216,128]{1,0:T(8,128)} custom-call(f32[256,256]{1,0:T(8,128)} %bitcast.2, s32[1,3]{1,0:T(1,128)} %partners_ref.1, bf16[384,256]{1,0:T(8,128)(2,1)} %constant.8.clone.first_ref, bf16[768,256]{1,0:T(8,128)(2,1)} %constant.9.clone.second_ref, bf16[768,256]{1,0:T(8,128)(2,1)} %constant.10.clone.third_ref), custom_call_target="tpu_custom_call" | custom-call | tf_op jit(solution)/shard_map/pallas_call | solution.py:250
  18.1 1.6 %broadcast_multiply_fusion = f32[216,128]{1,0:T(8,128)} fusion(f32[216,128]{1,0:T(8,128)} %shard_map.55), kind=kLoop, calls=%fused_computation | loop fusion | flops 27648 | bytes 221184 | tf_op jit(solution)/shard_map/mul | solution.py:272

commit v4 on v3

--- a/solution.py
+++ b/solution.py
@@ -134,7 +134,7 @@
                 def _():
                     send(c, slot, device, which).start()
 
-    start([sends[0], sends[2], (quick & sends[1][0],) + sends[1][1:]])
+    start([(even & sends[0][0],) + sends[0][1:], sends[2], (quick & sends[1][0],) + sends[1][1:]])
 
     def transform(read, into):
         def block(i, j):
@@ -196,9 +196,13 @@
         load.wait()
 
     def turn(step, carry):
-        odd_slot = jnp.where(step == REACH, 0, jnp.where(quick, REACH - step, step))
-        slot = jnp.where(step == 0, REACH, jnp.where(even, step - 1, odd_slot))
+        turned = jnp.where(odd & quick, lax.rem(step + 1, REACH), step - 1)
+        slot = jnp.where(step == 0, REACH, turned)
         here = (step == 0) | (me + slot + 1 < total)
+
+        @pl.when(step == 1)
+        def _():
+            start([(odd & sends[0][0],) + sends[0][1:]])
 
         @pl.when(step == 2)
         def _():

time: 19.8 us -> 19.3 us (0.975)
  the two profiles are of different devices: /device:TPU:1 before, /device:TPU:6 now
where the time goes in v4:
time: 19.3 us; the launch traced here: 19.1 us
  Pallas kernels  17.6 us (91%)
  other arithmetic  1.55 us (8%)
    pallas_call x1, Pallas kernels, body(): pl.pallas_call(functools.partial(kernel, total, grid), out_shape=jax.Shap...  17.6 us
    mul x1, other arithmetic, body(): result = lax.optimization_barrier(result * (1.0 / PATCH))  1.55 us

profile of v4, /device:TPU:6, one launch (start us, length us, event | category | flops | bytes accessed | tf_op | source)
XLA Modules:
  0.0 19.1 jit_solution(4881395919583348446)
XLA Ops:
  0.0 17.6 %shard_map.55 = f32[216,128]{1,0:T(8,128)} custom-call(f32[256,256]{1,0:T(8,128)} %bitcast.2, s32[1,3]{1,0:T(1,128)} %partners_ref.1, bf16[384,256]{1,0:T(8,128)(2,1)} %constant.8.clone.first_ref, bf16[768,256]{1,0:T(8,128)(2,1)} %constant.9.clone.second_ref, bf16[768,256]{1,0:T(8,128)(2,1)} %constant.10.clone.third_ref), custom_call_target="tpu_custom_call" | custom-call | tf_op jit(solution)/shard_map/pallas_call | solution.py:254
  17.6 1.6 %broadcast_multiply_fusion = f32[216,128]{1,0:T(8,128)} fusion(f32[216,128]{1,0:T(8,128)} %shard_map.55), kind=kLoop, calls=%fused_computation | loop fusion | flops 27648 | bytes 221184 | tf_op jit(solution)/shard_map/mul | solution.py:276

commit v5 on v3

--- a/solution.py
+++ b/solution.py
@@ -196,7 +196,7 @@
         load.wait()
 
     def turn(step, carry):
-        odd_slot = jnp.where(step == REACH, 0, jnp.where(quick, REACH - step, step))
+        odd_slot = jnp.where(quick, REACH - step, jnp.where(step == REACH, 2, 2 - step))
         slot = jnp.where(step == 0, REACH, jnp.where(even, step - 1, odd_slot))
         here = (step == 0) | (me + slot + 1 < total)
 

time: 19.8 us -> 18.7 us (0.944)
  Pallas kernels: 18.1 us -> 17 us
    pallas_call x1, Pallas kernels: 18.1 us -> 17 us  [body(): pl.pallas_call(functools.partial(kernel, total, grid), out_shape=jax.Shap...]
where the time goes in v5:
time: 18.7 us; the launch traced here: 18.6 us
  Pallas kernels  17 us (91%)
  other arithmetic  1.55 us (8%)
    pallas_call x1, Pallas kernels, body(): pl.pallas_call(functools.partial(kernel, total, grid), out_shape=jax.Shap...  17 us
    mul x1, other arithmetic, body(): result = lax.optimization_barrier(result * (1.0 / PATCH))  1.55 us

profile of v5, /device:TPU:1, one launch (start us, length us, event | category | flops | bytes accessed | tf_op | source)
XLA Modules:
  0.0 18.6 jit_solution(13800312378788509662)
XLA Ops:
  0.0 17.0 %shard_map.55 = f32[216,128]{1,0:T(8,128)} custom-call(f32[256,256]{1,0:T(8,128)} %bitcast.2, s32[1,3]{1,0:T(1,128)} %partners_ref.1, bf16[384,256]{1,0:T(8,128)(2,1)} %constant.8.clone.first_ref, bf16[768,256]{1,0:T(8,128)(2,1)} %constant.9.clone.second_ref, bf16[768,256]{1,0:T(8,128)(2,1)} %constant.10.clone.third_ref), custom_call_target="tpu_custom_call" | custom-call | tf_op jit(solution)/shard_map/pallas_call | solution.py:250
  17.0 1.6 %broadcast_multiply_fusion = f32[216,128]{1,0:T(8,128)} fusion(f32[216,128]{1,0:T(8,128)} %shard_map.55), kind=kLoop, calls=%fused_computation | loop fusion | flops 27648 | bytes 221184 | tf_op jit(solution)/shard_map/mul | solution.py:272

commit v6 on v5

--- a/solution.py
+++ b/solution.py
@@ -65,7 +65,8 @@
     return jnp.dot(a, b, preferred_element_type=jnp.float32)
 
 
-def kernel(total, grid, tile_ref, partners_ref, first_ref, second_ref, third_ref, out_ref,
+def kernel(total, grid, tile_ref, partners_ref, first_ref, second_ref, third_ref, result_ref,
+           out_ref, store_sem,
            partners, first, second, third, load_sem, slots, spectra, seg_h, seg_l, lined, send_sem, recv_sem, forward_sem):
     me = lax.axis_index("section")
     even = lax.rem(me, 2) == 0
@@ -192,7 +193,7 @@
                 line = jnp.where(lane == q, lined[pl.ds(g * per + q, grid * grid, stride=CROP)], line)
             out_ref[pl.ds(slot * lines + g, grid * grid, stride=CROP // per)] = jnp.where(listed, line, 0.0)
 
-    for load in loads:
+    for load in loads[:3]:
         load.wait()
 
     def turn(step, carry):
@@ -200,6 +201,11 @@
         slot = jnp.where(step == 0, REACH, jnp.where(even, step - 1, odd_slot))
         here = (step == 0) | (me + slot + 1 < total)
 
+        @pl.when(step == 1)
+        def _():
+            for load in loads[3:]:
+                load.wait()
+
         @pl.when(step == 2)
         def _():
             start([(jnp.logical_not(quick) & sends[1][0],) + sends[1][1:]])
@@ -224,9 +230,19 @@
         @pl.when(jnp.logical_not(here))
         def _():
             out_ref[pl.ds(pl.multiple_of(slot * lines, 8), lines)] = jnp.zeros((lines, PATCH), jnp.float32)
+
+        @pl.when(step > 0)
+        def _():
+            store(slot).start()
         return carry
 
+    def store(slot):
+        at = pl.ds(slot * lines, lines)
+        return pltpu.make_async_copy(out_ref.at[at], result_ref.at[at], store_sem.at[slot])
+
     lax.fori_loop(0, REACH + 1, turn, 0)
+    for slot in range(REACH):
+        store(slot).wait()
 
     for c in range(CHUNKS):
         for wanted, slot, device, which in sends:
@@ -246,13 +262,14 @@
     count = grid * grid
     lines = count * CROP * CROP // PATCH
     constants = tables()
-    vmem = pl.BlockSpec(memory_space=pltpu.VMEM)
     result = pl.pallas_call(
         functools.partial(kernel, total, grid),
         out_shape=jax.ShapeDtypeStruct((REACH * lines, PATCH), jnp.float32),
         in_specs=[pl.BlockSpec(memory_space=pltpu.HBM)] * 5,
-        out_specs=vmem,
+        out_specs=pl.BlockSpec(memory_space=pltpu.HBM),
         scratch_shapes=[
+            pltpu.VMEM((REACH * lines, PATCH), jnp.float32),
+            pltpu.SemaphoreType.DMA((REACH,)),
             pltpu.SMEM((1, REACH), jnp.int32),
             *[pltpu.VMEM(t.shape, BF) for t in constants],
             pltpu.SemaphoreType.DMA((5,)),

time: 18.7 us -> 18.7 us (level)
  no operation moved by 1% of the time
where the time goes in v6:
time: 18.7 us; the launch traced here: 18.6 us
  Pallas kernels  17 us (91%)
  other arithmetic  1.55 us (8%)
    pallas_call x1, Pallas kernels, body(): pl.pallas_call(functools.partial(kernel, total, grid), out_shape=jax.Shap...  17 us
    mul x1, other arithmetic, body(): result = lax.optimization_barrier(result * (1.0 / PATCH))  1.55 us

profile of v6, /device:TPU:1, one launch (start us, length us, event | category | flops | bytes accessed | tf_op | source)
XLA Modules:
  0.0 18.6 jit_solution(16461024743315707890)
XLA Ops:
  0.0 17.0 %shard_map.55 = f32[216,128]{1,0:T(8,128)} custom-call(f32[256,256]{1,0:T(8,128)} %bitcast.2, s32[1,3]{1,0:T(1,128)} %partners_ref.1, bf16[384,256]{1,0:T(8,128)(2,1)} %constant.8.clone.first_ref, bf16[768,256]{1,0:T(8,128)(2,1)} %constant.9.clone.second_ref, bf16[768,256]{1,0:T(8,128)(2,1)} %constant.10.clone.third_ref), custom_call_target="tpu_custom_call" | custom-call | tf_op jit(solution)/shard_map/pallas_call | solution.py:265
  17.0 1.6 %broadcast_multiply_fusion = f32[216,128]{1,0:T(8,128)} fusion(f32[216,128]{1,0:T(8,128)} %shard_map.55), kind=kLoop, calls=%fused_computation | loop fusion | flops 27648 | bytes 221184 | tf_op jit(solution)/shard_map/mul | solution.py:289

commit v7 on v6

--- a/solution.py
+++ b/solution.py
@@ -15,7 +15,7 @@
 CROP = 32
 HALF = PATCH // 2
 ROWS = 80
-CHUNKS = 2
+CHUNKS = 4
 BF = jnp.bfloat16
 
 

time: 18.7 us -> 18.9 us (1.011)
  Pallas kernels: 17 us -> 17.2 us
where the time goes in v7:
time: 18.9 us; the launch traced here: 18.7 us
  Pallas kernels  17.2 us (91%)
  other arithmetic  1.55 us (8%)
    pallas_call x1, Pallas kernels, body(): pl.pallas_call(functools.partial(kernel, total, grid), out_shape=jax.Shap...  17.2 us
    mul x1, other arithmetic, body(): result = lax.optimization_barrier(result * (1.0 / PATCH))  1.55 us

profile of v7, /device:TPU:1, one launch (start us, length us, event | category | flops | bytes accessed | tf_op | source)
XLA Modules:
  0.0 18.7 jit_solution(17097193218477633880)
XLA Ops:
  0.0 17.2 %shard_map.55 = f32[216,128]{1,0:T(8,128)} custom-call(f32[256,256]{1,0:T(8,128)} %bitcast.2, s32[1,3]{1,0:T(1,128)} %partners_ref.1, bf16[384,256]{1,0:T(8,128)(2,1)} %constant.8.clone.first_ref, bf16[768,256]{1,0:T(8,128)(2,1)} %constant.9.clone.second_ref, bf16[768,256]{1,0:T(8,128)(2,1)} %constant.10.clone.third_ref), custom_call_target="tpu_custom_call" | custom-call | tf_op jit(solution)/shard_map/pallas_call | solution.py:265
  17.2 1.6 %broadcast_multiply_fusion = f32[216,128]{1,0:T(8,128)} fusion(f32[216,128]{1,0:T(8,128)} %shard_map.55), kind=kLoop, calls=%fused_computation | loop fusion | flops 27648 | bytes 221184 | tf_op jit(solution)/shard_map/mul | solution.py:289
